TPU v7x, 32 devices: a whole 2x2x4 slice. The times are simulated.
32 devices in a mesh: ep: 32 (over z, y, x, core), dp: 1.
Axes of the slice: x: 2, y: 2, z: 4, core: 2. Of those that a mesh axis runs over, the one named last changes fastest.
Arguments:
- tokens: bfloat16 [768, 3584], P(('ep', 'dp')), may hold values from -6 to 6
- grad_out: bfloat16 [768, 3584], P(('ep', 'dp')), may hold values from -0.29882812 to 0.29882812
- routes: int32 [768, 2], P(('ep', 'dp')), may hold values from 0 to 3, all different within a row; in each aligned block of 24 rows (0 to 23, 24 to 47, ...) at most 16 rows name the same one
- route_probs: float32 [768, 2], P(('ep', 'dp')), may hold values from 0.1 to 1
- gate_weight: bfloat16 [32, 3584, 128], P('ep', 'dp'), may hold values from -0.09375 to 0.09375
- up_weight: bfloat16 [32, 3584, 128], P('ep', 'dp'), may hold values from -0.09375 to 0.09375
- down_weight: bfloat16 [32, 3584, 128], P('ep', 'dp'), may hold values from -0.1875 to 0.1875
Outputs:
- grad_tokens: bfloat16 [768, 3584], P(('ep', 'dp'))
- grad_probs: float32 [768, 2], P(('ep', 'dp'))
- grad_gate: bfloat16 [32, 3584, 128], P('ep', 'dp')
- grad_up: bfloat16 [32, 3584, 128], P('ep', 'dp')
- grad_down: bfloat16 [32, 3584, 128], P('ep', 'dp')
Inputs may be any that keep to these rules, and one draw needn't show every extreme that they name: `routes`: each row names 2 different experts. Within each aligned block of 24 rows (the tokens of one device) no expert is named by more than 16 rows; in some blocks one expert is named by exactly 16 rows.
All inputs are finite; a program needn't handle non-finite values.
Results may differ from a plain program's by a relative error of at most 0.017.
Values may be sent and summed in bfloat16 or wider, within the bound.
A program may use at most 64 MiB of HBM per device.

v0:
```python
import jax
import jax.numpy as jnp
from jax import lax
from jax.sharding import PartitionSpec as P

GROUP = 8
TOP = 2


CONTRACT_HIDDEN = (((1,), (1,)), ((), ()))
CONTRACT_ROWS = (((0,), (0,)), ((), ()))


def as_sent(array):

    def short(part):
        return part.astype(jnp.bfloat16) if part.dtype == jnp.float32 else part

    return jax.tree.map(short, array)


def from_partner(value, axis, distance):
    mask = 2**distance
    pairs = [(source, source ^ mask) for source in range(lax.axis_size(axis))]
    return lax.ppermute(value, axis, pairs)


def slot_layout(routes, experts, capacity):
    flat_routes = routes.reshape(-1)
    copies = flat_routes.shape[0]
    onehot = (flat_routes[:, None] == jnp.arange(experts, dtype=jnp.int32)[None, :]).astype(
        jnp.int32
    )
    earlier = jnp.cumsum(onehot, axis=0) - onehot
    slot_rank = jnp.sum(earlier * onehot, axis=1)
    slot_index = flat_routes * capacity + slot_rank
    slot_copy = jnp.full((experts * capacity,), copies, jnp.int32)
    slot_copy = slot_copy.at[slot_index].set(jnp.arange(copies, dtype=jnp.int32))
    return (slot_index, slot_copy)


def per_device(tokens, grad_out, routes, route_probs, gate_weight, up_weight, down_weight):
    tok_count, features = tokens.shape
    ep_size = lax.axis_size("ep")
    experts = ep_size // GROUP
    slots = min(
        tok_count // GROUP,
        max(1, (4 * TOP * tok_count + 3 * experts * GROUP - 1) // (3 * experts * GROUP)),
    )
    capacity = GROUP * slots
    copies = tok_count * TOP
    slot_index, slot_copy = slot_layout(routes, experts, capacity)
    source_row = jnp.where(slot_copy < copies, slot_copy // TOP, tok_count)
    blank = jnp.zeros((1, features), jnp.bfloat16)
    send_tokens = jnp.concatenate([tokens, blank], axis=0)[source_row]
    send_grads = jnp.concatenate([grad_out, blank], axis=0)[source_row]
    flat_probs = jnp.concatenate([route_probs.reshape(-1), jnp.zeros((1,), jnp.float32)])
    send_probs = flat_probs[slot_copy]
    position = lax.axis_index("ep")
    current = (
        lax.all_to_all(
            send_tokens.reshape(ep_size, slots, features),
            "ep",
            split_axis=0,
            concat_axis=0,
            tiled=True,
        ),
        lax.all_to_all(
            send_grads.reshape(ep_size, slots, features),
            "ep",
            split_axis=0,
            concat_axis=0,
            tiled=True,
        ),
        lax.all_to_all(
            send_probs.reshape(ep_size, slots).astype(jnp.bfloat16),
            "ep",
            split_axis=0,
            concat_axis=0,
            tiled=True,
        ).astype(jnp.float32),
    )
    for section_bit in range(GROUP.bit_length() - 1):
        partner = from_partner((current[0], current[1], as_sent(current[2])), "ep", section_bit)
        upper_half = position >> section_bit & 1 == 1
        merged = []
        for own_part, their_part in zip(current, partner):
            lower_part = jnp.where(upper_half, their_part, own_part)
            upper_part = jnp.where(upper_half, own_part, their_part)
            merged.append(jnp.concatenate([lower_part, upper_part], axis=1))
        current = tuple(merged)
    rows_tok, rows_grd, rows_prb = current
    rows_in = rows_tok.reshape(-1, features)
    rows_grad = rows_grd.reshape(-1, features)
    rows_prob = rows_prb.reshape(-1)
    gate_all, up_all, down_all = (
        lax.all_gather(gate_weight, "dp", axis=1, tiled=True),
        lax.all_gather(up_weight, "dp", axis=1, tiled=True),
        lax.all_gather(down_weight, "dp", axis=1, tiled=True),
    )
    gate_full = gate_all[0]
    up_full = up_all[0]
    down_full = down_all[0]
    gate_pre = jnp.dot(rows_in, gate_full, preferred_element_type=jnp.float32)
    up_pre = jnp.dot(rows_in, up_full, preferred_element_type=jnp.float32)
    sigmoid_gate = jax.nn.sigmoid(gate_pre)
    activated = gate_pre * sigmoid_gate
    hidden = (activated * up_pre).astype(jnp.bfloat16)
    scaled = (rows_prob[:, None] * rows_grad.astype(jnp.float32)).astype(jnp.bfloat16)
    down_grad = jnp.dot(rows_grad, down_full, preferred_element_type=jnp.float32)
    scores = jnp.sum(hidden.astype(jnp.float32) * down_grad, axis=1)
    hidden_grad = rows_prob[:, None] * down_grad
    gate_grad = (
        hidden_grad * up_pre * sigmoid_gate * (1.0 + gate_pre * (1.0 - sigmoid_gate))
    ).astype(jnp.bfloat16)
    up_grad = (hidden_grad * activated).astype(jnp.bfloat16)
    token_part = (
        lax.dot_general(gate_grad, gate_full, CONTRACT_HIDDEN, preferred_element_type=jnp.float32)
        + lax.dot_general(up_grad, up_full, CONTRACT_HIDDEN, preferred_element_type=jnp.float32)
    ).astype(jnp.bfloat16)
    returned, returned_scores = (
        lax.all_to_all(
            token_part.reshape(ep_size, capacity, features),
            "ep",
            split_axis=0,
            concat_axis=0,
            tiled=True,
        ),
        lax.all_to_all(
            scores.reshape(ep_size, capacity).astype(jnp.bfloat16),
            "ep",
            split_axis=0,
            concat_axis=0,
            tiled=True,
        ).astype(jnp.float32),
    )
    slot_rows = jnp.sum(
        returned.reshape(experts, GROUP, capacity, features), axis=1, dtype=jnp.float32
    ).reshape(experts * capacity, features)
    slot_scores = jnp.sum(returned_scores.reshape(experts, GROUP, capacity), axis=1).reshape(-1)
    gate_term = lax.dot_general(
        rows_in, gate_grad, CONTRACT_ROWS, preferred_element_type=jnp.float32
    )
    up_term = lax.dot_general(rows_in, up_grad, CONTRACT_ROWS, preferred_element_type=jnp.float32)
    down_term = lax.dot_general(scaled, hidden, CONTRACT_ROWS, preferred_element_type=jnp.float32)
    gate_sum, up_sum, down_sum = (
        lax.psum_scatter(
            gate_term.astype(jnp.bfloat16), "dp", scatter_dimension=0, tiled=True
        ).astype(jnp.float32),
        lax.psum_scatter(
            up_term.astype(jnp.bfloat16), "dp", scatter_dimension=0, tiled=True
        ).astype(jnp.float32),
        lax.psum_scatter(
            down_term.astype(jnp.bfloat16), "dp", scatter_dimension=0, tiled=True
        ).astype(jnp.float32),
    )
    grad_tokens = jnp.sum(slot_rows[slot_index].reshape(tok_count, TOP, features), axis=1).astype(
        jnp.bfloat16
    )
    grad_probs = slot_scores[slot_index].reshape(tok_count, TOP)
    grad_gate = gate_sum.astype(jnp.bfloat16)[None]
    grad_up = up_sum.astype(jnp.bfloat16)[None]
    grad_down = down_sum.astype(jnp.bfloat16)[None]
    return (grad_tokens, grad_probs, grad_gate, grad_up, grad_down)


def solution(mesh):
    placed = (
        P(("ep", "dp"), None),
        P(("ep", "dp"), None),
        P(("ep", "dp"), None),
        P(("ep", "dp"), None),
        P("ep", "dp", None),
        P("ep", "dp", None),
        P("ep", "dp", None),
    )
    return jax.shard_map(
        per_device,
        mesh=mesh,
        in_specs=placed,
        out_specs=(
            P(("ep", "dp"), None),
            P(("ep", "dp"), None),
            P("ep", "dp", None),
            P("ep", "dp", None),
            P("ep", "dp", None),
        ),
        check_vma=False,
    )
```

profile of v0, /device:TPU:0, one launch (start us, length us, event | category | flops | bytes accessed | tf_op | source)
XLA Modules:
  0.0 280.0 jit_solution(11224181608938906223)
XLA Ops:
  6.1 7.3 %all-to-all-start = ((bf16[32,1,2]{2,1,0:T(2,128)(2,1)}), bf16[32,1,2]{2,1,0:T(2,128)(2,1)S(1)}, u32[]{:S(2)}, u32[]{:S(2)}) async-start(bf16[32,1,2]{2,1,0:T(2,128)(2,1)} %convert_element_type.141), calls=%async_computation | async-start | bytes 32768 | tf_op jit(solution)/shard_map/all_to_all | solution.py:75
  16.1 4.4 %all-to-all-done = bf16[32,1,2]{2,1,0:T(2,128)(2,1)S(1)} async-done(((bf16[32,1,2]{2,1,0:T(2,128)(2,1)}), bf16[32,1,2]{2,1,0:T(2,128)(2,1)S(1)}, u32[]{:S(2)}, u32[]{:S(2)}) %all-to-all-start) | async-done | bytes 160 | tf_op jit(solution)/shard_map/all_to_all | solution.py:75
  20.5 2.6 all-to-all-start.2
  24.9 12.6 %all-to-all-done.2 = bf16[32,2,3584]{2,1,0:T(2,128)(2,1)S(1)} async-done(((bf16[32,2,3584]{2,1,0:T(2,128)(2,1)}), bf16[32,2,3584]{2,1,0:T(2,128)(2,1)S(1)}, u32[]{:S(2)}, u32[]{:S(2)}) %all-to-all-start.2) | async-done | bytes 458784 | tf_op jit(solution)/shard_map/all_to_all | solution.py:61
  37.4 2.9 %all-to-all-start.1 = ((bf16[32,2,3584]{2,1,0:T(2,128)(2,1)}), bf16[32,2,3584]{2,1,0:T(2,128)(2,1)S(1)}, u32[]{:S(2)}, u32[]{:S(2)}) async-start(bf16[32,2,3584]{2,1,0:T(2,128)(2,1)} %reshape.107), calls=%async_computation.1 | async-start | bytes 917504 | tf_op jit(solution)/shard_map/all_to_all | solution.py:68
  41.6 1.8 collective-permute-start.1
  43.4 1.8 collective-permute-done.1
  45.3 9.3 %all-to-all-done.1 = bf16[32,2,3584]{2,1,0:T(2,128)(2,1)S(1)} async-done(((bf16[32,2,3584]{2,1,0:T(2,128)(2,1)}), bf16[32,2,3584]{2,1,0:T(2,128)(2,1)S(1)}, u32[]{:S(2)}, u32[]{:S(2)}) %all-to-all-start.1) | async-done | bytes 458784 | tf_op jit(solution)/shard_map/all_to_all | solution.py:68
  55.6 1.2 collective-permute-start.7
  56.9 1.9 pad_maximum_fusion.4
  59.7 19.1 %collective-permute-done.7 = bf16[32,4,3584]{2,1,0:T(4,128)(2,1)S(1)} collective-permute-done((bf16[32,4,3584]{2,1,0:T(4,128)(2,1)S(1)}, bf16[32,4,3584]{2,1,0:T(4,128)(2,1)S(1)}, u32[]{:S(2)}, u32[]{:S(2)}) %collective-permute-start.7) | collective-permute-done | bytes 917536 | tf_op jit(solution)/shard_map/ppermute | solution.py:25
  78.8 1.4 broadcast_select_fusion.9
  80.2 2.1 pad_maximum_fusion.3
  84.5 39.5 %collective-permute-done.2 = bf16[32,8]{0,1:T(8,128)(2,1)S(1)} collective-permute-done((bf16[32,8]{0,1:T(8,128)(2,1)S(1)}, bf16[32,8]{0,1:T(8,128)(2,1)S(1)}, u32[]{:S(2)}, u32[]{:S(2)}) %collective-permute-start.2) | collective-permute-done | bytes 544 | tf_op jit(solution)/shard_map/ppermute | solution.py:25
  124.1 2.7 broadcast_select_fusion.11
  127.8 1.2 collective-permute-start.5
  129.0 2.8 %broadcast_select_fusion.1 = (bf16[32,8,3584]{2,1,0:T(8,128)(2,1)S(1)}, bf16[32,8,3584]{2,1,0:T(8,128)(2,1)S(1)}) fusion(bf16[32,8,3584]{2,1,0:T(8,128)(2,1)} %collective-permute-done.8, pred[]{:T(512)S(6)} %eq.24, bf16[32,4,3584]{2,1,0:T(4,128)(2,1)S(1)} %get-tuple-element.29, bf16[32,4,3584]{2,1,0:T(4,128)(2,1)S(1)} %get-tuple-element.28), kind=kLoop, calls=%fused_computation.21 | loop fusion | flops 5505024 | bytes 7340033 | tf_op jit(solution)/shard_map/jit(_where)/select_n | solution.py:88
  132.3 1.4 fusion.6
  134.1 1.4 fusion.9
  135.5 32.7 %collective-permute-done.5 = bf16[32,8,3584]{2,1,0:T(8,128)(2,1)S(1)} collective-permute-done((bf16[32,8,3584]{2,1,0:T(8,128)(2,1)S(1)}, bf16[32,8,3584]{2,1,0:T(8,128)(2,1)S(1)}, u32[]{:S(2)}, u32[]{:S(2)}) %collective-permute-start.5) | collective-permute-done | bytes 1835040 | tf_op jit(solution)/shard_map/ppermute | solution.py:25
  168.2 1.5 broadcast_select_fusion.3
  170.9 1.4 multiply_reduce_fusion
  172.3 4.1 %fusion.4 = f32[512,3584]{1,0:T(8,128)} fusion(bf16[512,128]{0,1:T(8,128)(2,1)S(1)} %get-tuple-element.34, bf16[1,3584,128]{2,1,0:T(8,128)(2,1)S(1)} %copy-done), kind=kOutput, calls=%fused_computation.26 | convolution fusion | flops 469762048 | bytes 8388608 | tf_op jit(solution)/shard_map/dot_general | solution.py:118
  177.1 2.9 %all-to-all-start.4 = ((bf16[32,1,16]{2,1,0:T(2,128)(2,1)}), bf16[32,1,16]{2,1,0:T(2,128)(2,1)S(1)}, u32[]{:S(2)}, u32[]{:S(2)}) async-start(bf16[32,1,16]{2,1,0:T(2,128)(2,1)} %convert_element_type.142), calls=%async_computation.4 | async-start | bytes 32768 | tf_op jit(solution)/shard_map/all_to_all | solution.py:129
  180.0 6.0 %add_convert_fusion = bf16[512,3584]{1,0:T(8,128)(2,1)} fusion(f32[512,3584]{1,0:T(8,128)} %fusion.4, bf16[512,128]{0,1:T(8,128)(2,1)S(1)} %get-tuple-element.35, bf16[1,3584,128]{2,1,0:T(8,128)(2,1)S(1)} %copy-done.4), kind=kOutput, calls=%fused_computation.8 | convolution fusion | flops 473432064 | bytes 12058624 | tf_op jit(solution)/shard_map/dot_general | solution.py:119
  187.1 4.9 %all-to-all-start.3 = ((bf16[32,16,3584]{2,1,0:T(8,128)(2,1)}), bf16[32,16,3584]{2,1,0:T(8,128)(2,1)}, u32[]{:S(2)}, u32[]{:S(2)}) async-start(bf16[32,16,3584]{2,1,0:T(8,128)(2,1)} %bitcast.63), calls=%async_computation.3 | async-start | bytes 7340032 | tf_op jit(solution)/shard_map/all_to_all | solution.py:122
  192.0 4.3 %fusion.1 = bf16[1,3584,128]{2,1,0:T(8,128)(2,1)} fusion(bf16[512,3584]{1,0:T(8,128)(2,1)} %bitcast.60, bf16[512,128]{0,1:T(8,128)(2,1)S(1)} %get-tuple-element.35), kind=kOutput, calls=%fused_computation.13 | convolution fusion | flops 470220800 | bytes 4718592 | tf_op jit(solution)/shard_map/dot_general | solution.py:144
  196.3 2.1 fusion
  198.4 2.5 fusion.2
  202.6 72.0 %all-to-all-done.3 = bf16[32,16,3584]{2,1,0:T(8,128)(2,1)} async-done(((bf16[32,16,3584]{2,1,0:T(8,128)(2,1)}), bf16[32,16,3584]{2,1,0:T(8,128)(2,1)}, u32[]{:S(2)}, u32[]{:S(2)}) %all-to-all-start.3) | async-done | bytes 3670048 | tf_op jit(solution)/shard_map/all_to_all | solution.py:122
  274.6 2.6 convert_reduce_fusion
  278.5 1.5 reduce_sum.50
  (79 shorter events, 23.0 us)
Async XLA Ops:
  0.6 131.7 %copy-start = (bf16[1,3584,128]{2,1,0:T(8,128)(2,1)S(1)}, bf16[1,3584,128]{2,1,0:T(8,128)(2,1)}, u32[]{:S(2)}) copy-start(bf16[1,3584,128]{2,1,0:T(8,128)(2,1)} %param.11) | copy-start | bytes 2752516
  0.6 22.4 %copy-start.7 = (bf16[24,3584]{1,0:T(8,128)(2,1)S(1)}, bf16[24,3584]{1,0:T(8,128)(2,1)}, u32[]{:S(2)}) copy-start(bf16[24,3584]{1,0:T(8,128)(2,1)} %param.8) | copy-start | bytes 516100
  6.1 14.4 %all-to-all-start = ((bf16[32,1,2]{2,1,0:T(2,128)(2,1)}), bf16[32,1,2]{2,1,0:T(2,128)(2,1)S(1)}, u32[]{:S(2)}, u32[]{:S(2)}) async-start(bf16[32,1,2]{2,1,0:T(2,128)(2,1)} %convert_element_type.141), calls=%async_computation | async-start | bytes 32768 | tf_op jit(solution)/shard_map/all_to_all | solution.py:75
  20.5 17.0 %all-to-all-start.2 = ((bf16[32,2,3584]{2,1,0:T(2,128)(2,1)}), bf16[32,2,3584]{2,1,0:T(2,128)(2,1)S(1)}, u32[]{:S(2)}, u32[]{:S(2)}) async-start(bf16[32,2,3584]{2,1,0:T(2,128)(2,1)} %reshape.109), calls=%async_computation.2 | async-start | bytes 917504 | tf_op jit(solution)/shard_map/all_to_all | solution.py:61
  37.4 17.1 %all-to-all-start.1 = ((bf16[32,2,3584]{2,1,0:T(2,128)(2,1)}), bf16[32,2,3584]{2,1,0:T(2,128)(2,1)S(1)}, u32[]{:S(2)}, u32[]{:S(2)}) async-start(bf16[32,2,3584]{2,1,0:T(2,128)(2,1)} %reshape.107), calls=%async_computation.1 | async-start | bytes 917504 | tf_op jit(solution)/shard_map/all_to_all | solution.py:68
  40.5 1.1 collective-permute-start
  40.7 13.8 %collective-permute-start.6 = (bf16[32,2,3584]{2,1,0:T(2,128)(2,1)S(1)}, bf16[32,2,3584]{2,1,0:T(2,128)(2,1)S(1)}, u32[]{:S(2)}, u32[]{:S(2)}) collective-permute-start(bf16[32,2,3584]{2,1,0:T(2,128)(2,1)S(1)} %all-to-all-done.2), channel_id=1, source_target_pairs={{0,1},{1,0},{2,3},{3,2},{4,5},{5,4},{6,7},{7,6},{8,9},{9,8},{10,11... | collective-permute-start | bytes 1376264 | tf_op jit(solution)/shard_map/ppermute | solution.py:25
  41.6 3.6 %collective-permute-start.1 = (bf16[32,4]{0,1:T(4,128)(2,1)S(1)}, bf16[32,4]{0,1:T(4,128)(2,1)S(1)}, u32[]{:S(2)}, u32[]{:S(2)}) collective-permute-start(bf16[32,4]{0,1:T(4,128)(2,1)S(1)} %fusion.16), channel_id=1, source_target_pairs={{0,2},{1,3},{2,0},{3,1},{4,6},{5,7},{6,4},{7,5},{8,10},{9,11},{10,... | collective-permute-start | bytes 776 | tf_op jit(solution)/shard_map/ppermute | solution.py:25
  54.5 2.2 collective-permute-start.3
  55.6 23.2 %collective-permute-start.7 = (bf16[32,4,3584]{2,1,0:T(4,128)(2,1)S(1)}, bf16[32,4,3584]{2,1,0:T(4,128)(2,1)S(1)}, u32[]{:S(2)}, u32[]{:S(2)}) collective-permute-start(bf16[32,4,3584]{2,1,0:T(4,128)(2,1)S(1)} %pad_maximum_fusion.5), channel_id=1, source_target_pairs={{0,2},{1,3},{2,0},{3,1},{4,6},{5,7},{6,4},{7,5},{8,10},{9,11},{10,... | collective-permute-start | bytes 2752520 | tf_op jit(solution)/shard_map/ppermute | solution.py:25
  56.9 2.8 copy-start.3
  58.8 65.3 %collective-permute-start.4 = (bf16[32,4,3584]{2,1,0:T(4,128)(2,1)}, bf16[32,4,3584]{2,1,0:T(4,128)(2,1)}, u32[]{:S(2)}, u32[]{:S(2)}) collective-permute-start(bf16[32,4,3584]{2,1,0:T(4,128)(2,1)} %pad_maximum_fusion.4), channel_id=1, source_target_pairs={{0,2},{1,3},{2,0},{3,1},{4,6},{5,7},{6,4},{7,5},{8,10},{9,11},{10,... | collective-permute-start | bytes 2752520 | tf_op jit(solution)/shard_map/ppermute | solution.py:25
  82.4 46.6 %collective-permute-start.8 = (bf16[32,8,3584]{2,1,0:T(8,128)(2,1)}, bf16[32,8,3584]{2,1,0:T(8,128)(2,1)}, u32[]{:S(2)}, u32[]{:S(2)}) collective-permute-start(bf16[32,8,3584]{2,1,0:T(8,128)(2,1)} %pad_maximum_fusion.3), channel_id=1, source_target_pairs={{0,4},{1,5},{2,6},{3,7},{4,0},{5,1},{6,2},{7,3},{8,12},{9,13},{10,... | collective-permute-start | bytes 5505032 | tf_op jit(solution)/shard_map/ppermute | solution.py:25
  83.5 40.4 %collective-permute-start.2 = (bf16[32,8]{0,1:T(8,128)(2,1)S(1)}, bf16[32,8]{0,1:T(8,128)(2,1)S(1)}, u32[]{:S(2)}, u32[]{:S(2)}) collective-permute-start(bf16[32,8]{0,1:T(8,128)(2,1)S(1)} %fusion.15), channel_id=1, source_target_pairs={{0,4},{1,5},{2,6},{3,7},{4,0},{5,1},{6,2},{7,3},{8,12},{9,13},{10,... | collective-permute-start | bytes 1544 | tf_op jit(solution)/shard_map/ppermute | solution.py:25
  127.8 40.4 %collective-permute-start.5 = (bf16[32,8,3584]{2,1,0:T(8,128)(2,1)S(1)}, bf16[32,8,3584]{2,1,0:T(8,128)(2,1)S(1)}, u32[]{:S(2)}, u32[]{:S(2)}) collective-permute-start(bf16[32,8,3584]{2,1,0:T(8,128)(2,1)S(1)} %pad_maximum_fusion.2), channel_id=1, source_target_pairs={{0,4},{1,5},{2,6},{3,7},{4,0},{5,1},{6,2},{7,3},{8,12},{9,13},{10,... | collective-permute-start | bytes 5505032 | tf_op jit(solution)/shard_map/ppermute | solution.py:25
  132.3 3.2 %copy-start.1 = (bf16[32,16,3584]{2,1,0:T(8,128)(2,1)}, bf16[32,16,3584]{2,1,0:T(8,128)(2,1)S(1)}, u32[]{:S(2)}) copy-start(bf16[32,16,3584]{2,1,0:T(8,128)(2,1)S(1)} %pad_maximum_fusion.1) | copy-start | bytes 11010052
  132.3 1.8 copy-start.4
  169.7 1.2 copy-start.8
  170.2 6.2 %copy-start.5 = (bf16[32,16,3584]{2,1,0:T(8,128)(2,1)}, bf16[32,16,3584]{2,1,0:T(8,128)(2,1)S(1)}, u32[]{:S(2)}) copy-start(bf16[32,16,3584]{2,1,0:T(8,128)(2,1)S(1)} %pad_maximum_fusion) | copy-start | bytes 11010052
  177.1 9.9 %all-to-all-start.4 = ((bf16[32,1,16]{2,1,0:T(2,128)(2,1)}), bf16[32,1,16]{2,1,0:T(2,128)(2,1)S(1)}, u32[]{:S(2)}, u32[]{:S(2)}) async-start(bf16[32,1,16]{2,1,0:T(2,128)(2,1)} %convert_element_type.142), calls=%async_computation.4 | async-start | bytes 32768 | tf_op jit(solution)/shard_map/all_to_all | solution.py:129
  187.1 87.6 %all-to-all-start.3 = ((bf16[32,16,3584]{2,1,0:T(8,128)(2,1)}), bf16[32,16,3584]{2,1,0:T(8,128)(2,1)}, u32[]{:S(2)}, u32[]{:S(2)}) async-start(bf16[32,16,3584]{2,1,0:T(8,128)(2,1)} %bitcast.63), calls=%async_computation.3 | async-start | bytes 7340032 | tf_op jit(solution)/shard_map/all_to_all | solution.py:122
  192.0 4.3 %copy-start.2 = (bf16[32,16,3584]{2,1,0:T(8,128)(2,1)S(1)}, bf16[32,16,3584]{2,1,0:T(8,128)(2,1)}, u32[]{:S(2)}) copy-start(bf16[32,16,3584]{2,1,0:T(8,128)(2,1)} %copy-done.1) | copy-start | bytes 11010052
  196.3 2.1 copy-start.6
where the time goes:
time: 281 us; the launch traced here: 280 us
  waiting for transfers between devices  193 us (69%)
  starting transfers between devices  28.3 us (10%)
  matrix products  23.2 us (8%)
  other arithmetic  20.9 us (7%)
  local copies, waits for them, and re-layouts  13.6 us (5%)
    ppermute x9, waiting for transfers between devices, from_partner(): return lax.ppermute(value, axis, pairs)  93.7 us
    all_to_all x1, waiting for transfers between devices, per_device(): lax.all_to_all(token_part.reshape(ep_size, capacity, features), 'ep', spl...  72 us
    all_to_all x1, waiting for transfers between devices, per_device(): lax.all_to_all(send_tokens.reshape(ep_size, slots, features), 'ep', split...  12.6 us
    all_to_all x1, waiting for transfers between devices, per_device(): lax.all_to_all(send_grads.reshape(ep_size, slots, features), 'ep', split_...  9.3 us
    select_n x9, other arithmetic, per_device(): lower_part = jnp.where(upper_half, their_part, own_part)  8.69 us
    ppermute x9, starting transfers between devices, from_partner(): return lax.ppermute(value, axis, pairs)  7.73 us
    all_to_all x1, starting transfers between devices, per_device(): lax.all_to_all(send_probs.reshape(ep_size, slots).astype(jnp.bfloat16), '...  7.3 us
    concatenate x7, other arithmetic, per_device(): merged.append(jnp.concatenate([lower_part, upper_part], axis=1))  6.81 us
  transfers between devices with their start and end apart: 14, of which 10 were waited for; matrix products, arithmetic and copies ran while one was open for 13% of the time, Pallas kernels for 0%

commit v1 on v0

v1 whole, which is shorter than its diff:
```python
import functools

import jax
import jax.numpy as jnp
from jax import lax
from jax.experimental import pallas as pl
from jax.experimental.pallas import tpu as pltpu
from jax.sharding import PartitionSpec as P

GROUP = 8
TOP = 2
LANES = 128
ROWS = 16
F32 = jnp.float32
BF16 = jnp.bfloat16
MESH = pl.DeviceIdType.MESH


def dot(a, b, ca, cb):
    return lax.dot_general(a, b, (((ca,), (cb,)), ((), ())), preferred_element_type=F32)


def fwd_label(k, kind):
    return k * 16 + kind


def kernel(
    experts,
    cap,
    tokens,
    grads,
    routes,
    probs,
    wg_hbm,
    wu_hbm,
    wd_hbm,
    out_tokens,
    out_probs,
    out_gate,
    out_up,
    out_down,
    xs,
    gs,
    x,
    g,
    sc,
    t,
    rcore,
    rxa,
    rxb,
    rya,
    ryb,
    rf1,
    rf2,
    o,
    wgu,
    wd,
    gut,
    hid,
    wsem,
    ssem,
    rsem,
):
    feats = tokens.shape[1]
    wide = feats + LANES
    r = experts * cap
    h1 = (wide // LANES + 1) // 2 * LANES
    hidden = wd.shape[1]
    me = lax.axis_index("ep")
    z = me // GROUP
    m = me % GROUP
    core = m % 2
    chip = m // 2
    xbit = chip % 2
    ybit = chip // 2
    chip_x = ybit * 2 + (1 - xbit)
    chip_y = (1 - ybit) * 2 + xbit
    chip_d = (1 - ybit) * 2 + (1 - xbit)
    base = z * GROUP
    dev_c = base + chip * 2 + (1 - core)
    dev_x = base + chip_x * 2 + core
    dev_y = base + chip_y * 2 + core

    def zof(k):
        val = z
        bit = 1
        while bit < experts:
            if k & bit:
                val = val + bit - 2 * bit * ((z // bit) % 2)
            bit *= 2
        return val

    zs = [zof(k) for k in range(experts)]
    dev_z = [zs[k] * GROUP + m for k in range(experts)]

    loads = [
        pltpu.make_async_copy(wg_hbm, wgu.at[:, pl.ds(0, hidden)], wsem.at[0]),
        pltpu.make_async_copy(wu_hbm, wgu.at[:, pl.ds(hidden, hidden)], wsem.at[1]),
        pltpu.make_async_copy(wd_hbm, wd, wsem.at[2]),
    ]
    for c in loads:
        c.start()

    barrier = pltpu.get_barrier_semaphore()
    friends = [dev_c, dev_x, dev_y] + dev_z[1:]
    for d in friends:
        pl.semaphore_signal(barrier, inc=1, device_id={"ep": d}, device_id_type=MESH)

    toks = tokens.shape[0]
    col = lax.broadcasted_iota(jnp.int32, (toks, r), 1)
    cole = col // cap
    cols = (col % cap).astype(F32)
    on0 = routes[:, 0:1] == cole
    on1 = routes[:, 1:2] == cole
    named = jnp.where(on0 | on1, 1.0, 0.0).astype(F32)
    lower = jnp.where(
        lax.broadcasted_iota(jnp.int32, (toks, toks), 1)
        < lax.broadcasted_iota(jnp.int32, (toks, toks), 0),
        1.0,
        0.0,
    ).astype(BF16)
    rank = dot(lower, named.astype(BF16), 1, 0)
    place = jnp.where(rank == cols, named, 0.0)
    place16 = place.astype(BF16)
    weight = place * (jnp.where(on0, probs[:, 0:1], 0.0) + jnp.where(on1, probs[:, 1:2], 0.0))
    high = weight.astype(BF16)
    low = (weight - high.astype(F32)).astype(BF16)
    ones = jnp.ones((toks, LANES), BF16)
    lane = lax.broadcasted_iota(jnp.int32, (r, LANES), 1)
    xs[:, :feats] = dot(place16, tokens[...], 0, 0).astype(BF16)
    xs[:, feats:] = jnp.where(lane < LANES // 2, dot(high, ones, 0, 0), dot(low, ones, 0, 0)).astype(BF16)
    gs[...] = dot(place16, grads[...], 0, 0).astype(BF16)

    started = []

    def send(label, src, dst, device):
        c = pltpu.make_async_remote_copy(
            src_ref=src,
            dst_ref=dst,
            send_sem=ssem.at[label],
            recv_sem=rsem.at[label],
            device_id={"ep": device},
            device_id_type=MESH,
        )
        c.start()
        started.append(c)
        return c

    def rows(zk, of_core):
        return pl.ds(pl.multiple_of(of_core * r + zk * cap, ROWS), cap)

    def slot(zk):
        return pl.ds(pl.multiple_of(zk * cap, ROWS), cap)

    pl.semaphore_wait(barrier, len(friends))

    first = {}
    for k in range(1, experts):
        there = rows(z, core)
        first[k] = (
            send(fwd_label(k, 0), xs.at[slot(zs[k])], x.at[chip, there], dev_z[k]),
            send(fwd_label(k, 1), gs.at[slot(zs[k])], g.at[chip, there], dev_z[k]),
        )
    x[chip, rows(z, core), :] = xs[slot(z), :]
    g[chip, rows(z, core), :] = gs[slot(z), :]

    own, diag, fromcore = {}, {}, {}
    for step in range(experts + 2):
        k = step
        if k < experts:
            if k > 0:
                first[k][0].wait_recv()
                first[k][1].wait_recv()
            at = rows(zs[k], core)
            xr, gr = x.at[chip, at], g.at[chip, at]
            own[k] = (
                send(fwd_label(k, 2), xr, xr, dev_x),
                send(fwd_label(k, 5), gr, gr, dev_y),
                send(fwd_label(k, 3), gr, gr, dev_x),
                send(fwd_label(k, 4), xr, xr, dev_y),
            )
            fromcore[0, k] = (
                send(fwd_label(k, 6), xr, xr, dev_c),
                send(fwd_label(k, 7), gr, gr, dev_c),
            )
        k = step - 1
        if 0 <= k < experts:
            at = rows(zs[k], core)
            xx, gx = x.at[chip_x, at], g.at[chip_x, at]
            xy, gy = x.at[chip_y, at], g.at[chip_y, at]
            own[k][0].wait_recv()
            dx = send(fwd_label(k, 8), xx, xx, dev_y)
            own[k][1].wait_recv()
            dg = send(fwd_label(k, 9), gy, gy, dev_x)
            own[k][2].wait_recv()
            own[k][3].wait_recv()
            diag[k] = (dx, dg)
            fromcore[1, k] = (
                send(fwd_label(k, 10), xx, xx, dev_c),
                send(fwd_label(k, 11), gx, gx, dev_c),
            )
            fromcore[2, k] = (
                send(fwd_label(k, 12), xy, xy, dev_c),
                send(fwd_label(k, 13), gy, gy, dev_c),
            )
        k = step - 2
        if 0 <= k < experts:
            at = rows(zs[k], core)
            xd, gd = x.at[chip_d, at], g.at[chip_d, at]
            diag[k][0].wait_recv()
            diag[k][1].wait_recv()
            fromcore[3, k] = (
                send(fwd_label(k, 14), xd, xd, dev_c),
                send(fwd_label(k, 15), gd, gd, dev_c),
            )

    for c in loads:
        c.wait()

    tile = 512 if feats % 512 == 0 else LANES
    n_tiles = feats // tile
    chips = (chip, chip_x, chip_y, chip_d)
    back = experts * 16
    cores = {}
    for q in (3, 1, 2, 0):
        for k in range(experts):
            for c in fromcore[q, k]:
                c.wait_recv()
        cq = chips[q]
        pre = dot(x[cq, :, :feats], wgu[...], 1, 0)
        down = dot(g[cq], wd[...], 1, 0)
        tail = x[cq, :, feats:].astype(F32)
        prob = tail[:, 0:1] + tail[:, LANES // 2 : LANES // 2 + 1]
        gate, up = pre[:, :hidden], pre[:, hidden:]
        sig = jax.nn.sigmoid(gate)
        act = gate * sig
        hid_q = (act * up).astype(BF16)
        score = jnp.sum(hid_q.astype(F32) * down, axis=1, keepdims=True)
        hg = prob * down
        ggrad = (hg * up * sig * (1.0 + gate * (1.0 - sig))).astype(BF16)
        ugrad = (hg * act).astype(BF16)
        both = jnp.concatenate([ggrad, ugrad], axis=1)
        t[cq, :, feats:] = jnp.broadcast_to(score, (2 * r, LANES)).astype(BF16)
        lanes = pl.ds(pl.multiple_of(cq * (2 * r), LANES), 2 * r)
        gut[:, lanes] = both.T
        hid[:, lanes] = hid_q.T

        def part(i, _):
            at = pl.ds(pl.multiple_of(i * tile, tile), tile)
            t[cq, :, at] = dot(both, wgu[at, :], 1, 1).astype(BF16)
            sc[cq, :, at] = (prob * g[cq, :, at].astype(F32)).astype(BF16)
            return 0

        lax.fori_loop(0, n_tiles, part, 0)
        away = pl.ds(pl.multiple_of((1 - core) * r, ROWS), r)
        cores[q] = send(back + q, t.at[cq, away], rcore.at[q], dev_c)

    left = pl.ds(0, h1)
    right = pl.ds(h1, wide - h1)
    back += 4
    hop1, hop2, home = {}, {}, {}
    for q in (3, 1, 2):
        cores[q].wait_recv()
    for k in range(experts - 1, -1, -1):
        at, zk = rows(zs[k], core), slot(zs[k])
        for q in (3, 1, 2):
            t[chips[q], at, :] = (
                t[chips[q], at, :].astype(F32) + rcore[q, zk, :].astype(F32)
            ).astype(BF16)
        b = back + 8 * k
        hop1[k] = (
            send(b, t.at[chip_d, at, left], rxb.at[zk], dev_x),
            send(b + 1, t.at[chip_d, at, right], ryb.at[zk], dev_y),
            send(b + 2, t.at[chip_x, at, left], rxa.at[zk], dev_x),
            send(b + 3, t.at[chip_y, at, right], rya.at[zk], dev_y),
        )

    def wgrad(i, _):
        at = pl.ds(pl.multiple_of(i * tile, tile), tile)
        res = dot(gut[...], x[:, :, at].reshape(8 * r, tile), 1, 0).astype(BF16).T
        out_gate[at, :] = res[:, :hidden]
        out_up[at, :] = res[:, hidden:]
        return 0

    lax.fori_loop(0, n_tiles, wgrad, 0)
    for k in range(experts - 1, -1, -1):
        at, zk = rows(zs[k], core), slot(zs[k])
        b = back + 8 * k
        hop1[k][0].wait_recv()
        t[chip_y, at, left] = (t[chip_y, at, left].astype(F32) + rxb[zk, :].astype(F32)).astype(BF16)
        s1 = send(b + 4, t.at[chip_y, at, left], rf1.at[zk], dev_y)
        hop1[k][1].wait_recv()
        t[chip_x, at, right] = (t[chip_x, at, right].astype(F32) + ryb[zk, :].astype(F32)).astype(BF16)
        s2 = send(b + 5, t.at[chip_x, at, right], rf2.at[zk], dev_x)
        hop2[k] = (s1, s2)

    def dgrad(i, _):
        at = pl.ds(pl.multiple_of(i * tile, tile), tile)
        out_down[at, :] = dot(hid[...], sc[:, :, at].reshape(8 * r, tile), 1, 0).astype(BF16).T
        return 0

    lax.fori_loop(0, n_tiles, dgrad, 0)
    cores[0].wait_recv()
    for k in range(experts - 1, -1, -1):
        at, zk = rows(zs[k], core), slot(zs[k])
        for c in (hop1[k][2], hop1[k][3], hop2[k][0], hop2[k][1]):
            c.wait_recv()
        mine = t[chip, at, :].astype(F32) + rcore[0, zk, :].astype(F32)
        lo = mine[:, :h1] + rxa[zk, :].astype(F32) + rf1[zk, :].astype(F32)
        hi = mine[:, h1:] + rya[zk, :].astype(F32) + rf2[zk, :].astype(F32)
        if k > 0:
            t[chip, at, left] = lo.astype(BF16)
            t[chip, at, right] = hi.astype(BF16)
            home[k] = send(back + 8 * k + 6, t.at[chip, at], o.at[slot(z)], dev_z[k])
        else:
            o[zk, left] = lo.astype(BF16)
            o[zk, right] = hi.astype(BF16)
    for k in range(1, experts):
        home[k].wait_recv()
    out_tokens[...] = dot(place16, o[:, :feats], 1, 0).astype(BF16)
    scores = o[:, feats:]
    s0 = dot(jnp.where(on0, place, 0.0).astype(BF16), scores, 1, 0)
    s1 = dot(jnp.where(on1, place, 0.0).astype(BF16), scores, 1, 0)
    lane = lax.broadcasted_iota(jnp.int32, (toks, LANES), 1)
    out_probs[...] = jnp.where(lane == 0, s0, s1)
    for c in started:
        c.wait_send()


def expert_call(experts, cap, tokens, grads, routes, probs, wg, wu, wd):
    toks, feats = tokens.shape
    hidden = wg.shape[1]
    r = experts * cap
    wide = feats + LANES
    h1 = (wide // LANES + 1) // 2 * LANES
    h2 = wide - h1
    vmem = pl.BlockSpec(memory_space=pltpu.VMEM)
    hbm = pl.BlockSpec(memory_space=pl.ANY)
    n_sem = experts * 16 + 4 + 8 * experts
    grad = jax.ShapeDtypeStruct((feats, hidden), BF16)
    return pl.pallas_call(
        functools.partial(kernel, experts, cap),
        out_shape=(
            jax.ShapeDtypeStruct((toks, feats), BF16),
            jax.ShapeDtypeStruct((toks, LANES), F32),
            grad,
            grad,
            grad,
        ),
        in_specs=[vmem] * 4 + [hbm] * 3,
        out_specs=(vmem,) * 5,
        scratch_shapes=[
            pltpu.VMEM((r, wide), BF16),
            pltpu.VMEM((r, feats), BF16),
            pltpu.VMEM((4, 2 * r, wide), BF16),
            pltpu.VMEM((4, 2 * r, feats), BF16),
            pltpu.VMEM((4, 2 * r, feats), BF16),
            pltpu.VMEM((4, 2 * r, wide), BF16),
            pltpu.VMEM((4, r, wide), BF16),
            pltpu.VMEM((r, h1), BF16),
            pltpu.VMEM((r, h1), BF16),
            pltpu.VMEM((r, h2), BF16),
            pltpu.VMEM((r, h2), BF16),
            pltpu.VMEM((r, h1), BF16),
            pltpu.VMEM((r, h2), BF16),
            pltpu.VMEM((r, wide), BF16),
            pltpu.VMEM((feats, 2 * hidden), BF16),
            pltpu.VMEM((feats, hidden), BF16),
            pltpu.VMEM((2 * hidden, 8 * r), BF16),
            pltpu.VMEM((hidden, 8 * r), BF16),
            pltpu.SemaphoreType.DMA((3,)),
            pltpu.SemaphoreType.DMA((n_sem,)),
            pltpu.SemaphoreType.DMA((n_sem,)),
        ],
        compiler_params=pltpu.CompilerParams(
            collective_id=0, has_side_effects=True, vmem_limit_bytes=58 * 2**20
        ),
    )(tokens, grads, routes, probs, wg, wu, wd)


def per_device(tokens, grad_out, routes, route_probs, gate_weight, up_weight, down_weight):
    tok_count = tokens.shape[0]
    experts = lax.axis_size("ep") // GROUP
    slots = min(
        tok_count // GROUP,
        max(1, (4 * TOP * tok_count + 3 * experts * GROUP - 1) // (3 * experts * GROUP)),
    )
    cap = -(-GROUP * slots // ROWS) * ROWS
    split = lax.axis_size("dp") > 1

    def whole(w):
        return lax.all_gather(w, "dp", axis=1, tiled=True)[0] if split else w[0]

    def shared(term):
        if split:
            term = lax.psum_scatter(term, "dp", scatter_dimension=0, tiled=True)
        return term.astype(BF16)[None]

    grad_tokens, probs, gate, up, down = expert_call(
        experts,
        cap,
        tokens,
        grad_out,
        routes,
        route_probs,
        whole(gate_weight),
        whole(up_weight),
        whole(down_weight),
    )
    return (grad_tokens, probs[:, :TOP], shared(gate), shared(up), shared(down))


def solution(mesh):
    rows = P(("ep", "dp"), None)
    blocks = P("ep", "dp", None)
    return jax.shard_map(
        per_device,
        mesh=mesh,
        in_specs=(rows,) * 4 + (blocks,) * 3,
        out_specs=(rows,) * 2 + (blocks,) * 3,
        check_vma=False,
    )
```

time: 281 us -> 91.6 us (0.33)
  waiting for transfers between devices: 193 us -> 0 us
  Pallas kernels: 0 us -> 80.9 us
  starting transfers between devices: 28.3 us -> 0 us
  matrix products: 23.2 us -> 0 us
  other arithmetic: 20.9 us -> 0 us
  local copies, waits for them, and re-layouts: 13.6 us -> 9.65 us
    all_to_all x5 -> x0, waiting for transfers between devices: 99.3 us -> none  [the longest x1 72 us: per_device(): lax.all_to_all(token_part.reshape(ep_size, capacity, features), 'ep', spl...]
    ppermute x9 -> x0, waiting for transfers between devices: 93.7 us -> none  [from_partner(): return lax.ppermute(value, axis, pairs)]
    pallas_call x0 -> x1, Pallas kernels: none -> 80.9 us  [expert_call(): pl.pallas_call(functools.partial(kernel, experts, cap), out_shape=(jax.Sh...]
    dot_general x8 -> x0, matrix products: 23.2 us -> none  [the longest x1 6.05 us: per_device(): lax.dot_general(up_grad, up_full, CONTRACT_HIDDEN, preferred_element_type...]
    all_to_all x5 -> x0, starting transfers between devices: 20.6 us -> none  [the longest x1 7.3 us: per_device(): lax.all_to_all(send_probs.reshape(ep_size, slots).astype(jnp.bfloat16), '...]
    select_n x11 -> x0, other arithmetic: 8.71 us -> none  [the longest x9 8.69 us: per_device(): lower_part = jnp.where(upper_half, their_part, own_part)]
    ppermute x9 -> x0, starting transfers between devices: 7.73 us -> none  [from_partner(): return lax.ppermute(value, axis, pairs)]
    concatenate x8 -> x0, other arithmetic: 6.88 us -> none  [the longest x7 6.81 us: per_device(): merged.append(jnp.concatenate([lower_part, upper_part], axis=1))]
  transfers between devices with their start and end apart: 14 -> 0, of which waited for: 10 -> 0; matrix products, arithmetic and copies ran while one was open for 13% -> 0% of each run, Pallas kernels for 0% -> 0%
where the time goes in v1:
time: 91.6 us; the launch traced here: 91.2 us
  Pallas kernels  80.9 us (88%)
  local copies, waits for them, and re-layouts  9.65 us (11%)
    pallas_call x1, Pallas kernels, expert_call(): pl.pallas_call(functools.partial(kernel, experts, cap), out_shape=(jax.Sh...  80.9 us
    unnamed x17, local copies, waits for them, and re-layouts  9.65 us

profile of v1, /device:TPU:0, one launch (start us, length us, event | category | flops | bytes accessed | tf_op | source)
XLA Modules:
  0.0 91.2 jit_solution(17403444587495917476)
XLA Ops:
  0.6 0.0 copy-start.3
  0.6 0.7 copy-done.3
  1.3 0.0 copy-start.4
  1.3 0.7 copy.12.routes
  2.0 0.0 copy-done.4
  2.0 0.7 copy.13.probs
  2.7 80.9 %shard_map.110 = (bf16[24,3584]{1,0:T(8,128)(2,1)}, f32[24,128]{1,0:T(8,128)}, bf16[3584,128]{1,0:T(8,128)(2,1)}, bf16[3584,128]{1,0:T(8,128)(2,1)}, bf16[3584,128]{1,0:T(8,128)(2,1)}) custom-call(bf16[24,3584]{1,0:T(8,128)(2,1)} %tokens.1, bf16[24,3584]{1,0:T(8,128)(2,1)} %grads.1, s32[24,2]{1,0:T(8,128)} %copy.12.routes, f32[24,2]{1,0:T(8,128)} %copy.13.probs, ...), custom_call_target="tpu_custom_call" | custom-call | tf_op jit(solution)/shard_map/pallas_call | solution.py:341
  83.6 0.0 copy-start.2
  83.6 0.7 copy-done.2
  84.3 0.6 copy.14
  84.9 1.6 %copy.19 = bf16[24,3584]{1,0:T(8,128)(2,1)} copy(bf16[24,3584]{1,0:T(8,128)(2,1)} %get-tuple-element.25) | data formatting | bytes 344064
  86.5 0.0 copy-start.1
  86.5 2.2 %copy.20 = bf16[1,3584,128]{2,1,0:T(8,128)(2,1)} copy(bf16[1,3584,128]{2,1,0:T(8,128)(2,1)} %bitcast.9) | data formatting | bytes 1835008
  88.8 0.0 copy-done.1
  88.8 0.0 copy-start
  88.8 0.9 %copy.21 = bf16[1,3584,128]{2,1,0:T(8,128)(2,1)} copy(bf16[1,3584,128]{2,1,0:T(8,128)(2,1)S(1)} %bitcast.8) | data formatting | bytes 1835008
  89.7 0.6 copy-done
  90.3 0.9 %copy.22 = bf16[1,3584,128]{2,1,0:T(8,128)(2,1)} copy(bf16[1,3584,128]{2,1,0:T(8,128)(2,1)S(1)} %bitcast.7) | data formatting | bytes 1835008
Async XLA Ops:
  0.6 0.7 copy-start.3
  1.3 0.7 copy-start.4
  83.6 0.7 copy-start.2
  86.5 2.2 %copy-start.1 = (bf16[3584,128]{1,0:T(8,128)(2,1)S(1)}, bf16[3584,128]{1,0:T(8,128)(2,1)}, u32[]{:S(2)}) copy-start(bf16[3584,128]{1,0:T(8,128)(2,1)} %get-tuple-element.13) | copy-start | bytes 2752516
  88.8 1.5 %copy-start = (bf16[3584,128]{1,0:T(8,128)(2,1)S(1)}, bf16[3584,128]{1,0:T(8,128)(2,1)}, u32[]{:S(2)}) copy-start(bf16[3584,128]{1,0:T(8,128)(2,1)} %get-tuple-element.14) | copy-start | bytes 2752516

commit v2 on v1

--- a/solution.py
+++ b/solution.py
@@ -27,10 +27,10 @@
 def kernel(
     experts,
     cap,
-    tokens,
-    grads,
-    routes,
-    probs,
+    tokens_hbm,
+    grads_hbm,
+    routes_hbm,
+    probs_hbm,
     wg_hbm,
     wu_hbm,
     wd_hbm,
@@ -57,6 +57,10 @@
     wd,
     gut,
     hid,
+    tokens,
+    grads,
+    routes,
+    probs,
     wsem,
     ssem,
     rsem,
@@ -93,6 +97,14 @@
     zs = [zof(k) for k in range(experts)]
     dev_z = [zs[k] * GROUP + m for k in range(experts)]
 
+    inputs = [
+        pltpu.make_async_copy(routes_hbm, routes, wsem.at[3]),
+        pltpu.make_async_copy(probs_hbm, probs, wsem.at[4]),
+        pltpu.make_async_copy(tokens_hbm, tokens, wsem.at[5]),
+        pltpu.make_async_copy(grads_hbm, grads, wsem.at[6]),
+    ]
+    for c in inputs:
+        c.start()
     loads = [
         pltpu.make_async_copy(wg_hbm, wgu.at[:, pl.ds(0, hidden)], wsem.at[0]),
         pltpu.make_async_copy(wu_hbm, wgu.at[:, pl.ds(hidden, hidden)], wsem.at[1]),
@@ -106,30 +118,31 @@
     for d in friends:
         pl.semaphore_signal(barrier, inc=1, device_id={"ep": d}, device_id_type=MESH)
 
+    for c in inputs:
+        c.wait()
     toks = tokens.shape[0]
-    col = lax.broadcasted_iota(jnp.int32, (toks, r), 1)
-    cole = col // cap
-    cols = (col % cap).astype(F32)
-    on0 = routes[:, 0:1] == cole
-    on1 = routes[:, 1:2] == cole
+    slot_at = lax.broadcasted_iota(jnp.int32, (r, toks), 0)
+    expert_at = slot_at // cap
+    on0 = routes[0:1, :] == expert_at
+    on1 = routes[1:2, :] == expert_at
     named = jnp.where(on0 | on1, 1.0, 0.0).astype(F32)
-    lower = jnp.where(
-        lax.broadcasted_iota(jnp.int32, (toks, toks), 1)
-        < lax.broadcasted_iota(jnp.int32, (toks, toks), 0),
+    upper = jnp.where(
+        lax.broadcasted_iota(jnp.int32, (toks, toks), 0)
+        < lax.broadcasted_iota(jnp.int32, (toks, toks), 1),
         1.0,
         0.0,
     ).astype(BF16)
-    rank = dot(lower, named.astype(BF16), 1, 0)
-    place = jnp.where(rank == cols, named, 0.0)
+    rank = dot(named.astype(BF16), upper, 1, 0)
+    place = jnp.where(rank == (slot_at % cap).astype(F32), named, 0.0)
     place16 = place.astype(BF16)
-    weight = place * (jnp.where(on0, probs[:, 0:1], 0.0) + jnp.where(on1, probs[:, 1:2], 0.0))
-    high = weight.astype(BF16)
-    low = (weight - high.astype(F32)).astype(BF16)
-    ones = jnp.ones((toks, LANES), BF16)
+    weight = place * jnp.where(on0, probs[0:1, :], probs[1:2, :])
+    prob_of = jnp.sum(weight, axis=1, keepdims=True)
+    high = prob_of.astype(BF16)
+    low = (prob_of - high.astype(F32)).astype(BF16)
     lane = lax.broadcasted_iota(jnp.int32, (r, LANES), 1)
-    xs[:, :feats] = dot(place16, tokens[...], 0, 0).astype(BF16)
-    xs[:, feats:] = jnp.where(lane < LANES // 2, dot(high, ones, 0, 0), dot(low, ones, 0, 0)).astype(BF16)
-    gs[...] = dot(place16, grads[...], 0, 0).astype(BF16)
+    xs[:, :feats] = dot(place16, tokens[...], 1, 0).astype(BF16)
+    xs[:, feats:] = jnp.where(lane < LANES // 2, high.astype(F32), low.astype(F32)).astype(BF16)
+    gs[...] = dot(place16, grads[...], 1, 0).astype(BF16)
 
     started = []
 
@@ -155,74 +168,77 @@
     pl.semaphore_wait(barrier, len(friends))
 
     first = {}
-    for k in range(1, experts):
+
+    def exchange(k):
         there = rows(z, core)
         first[k] = (
             send(fwd_label(k, 0), xs.at[slot(zs[k])], x.at[chip, there], dev_z[k]),
             send(fwd_label(k, 1), gs.at[slot(zs[k])], g.at[chip, there], dev_z[k]),
         )
+
+    for k in range(1, min(3, experts)):
+        exchange(k)
     x[chip, rows(z, core), :] = xs[slot(z), :]
     g[chip, rows(z, core), :] = gs[slot(z), :]
 
     own, diag, fromcore = {}, {}, {}
-    for step in range(experts + 2):
-        k = step
-        if k < experts:
-            if k > 0:
-                first[k][0].wait_recv()
-                first[k][1].wait_recv()
-            at = rows(zs[k], core)
-            xr, gr = x.at[chip, at], g.at[chip, at]
-            own[k] = (
-                send(fwd_label(k, 2), xr, xr, dev_x),
-                send(fwd_label(k, 5), gr, gr, dev_y),
-                send(fwd_label(k, 3), gr, gr, dev_x),
-                send(fwd_label(k, 4), xr, xr, dev_y),
-            )
-            fromcore[0, k] = (
-                send(fwd_label(k, 6), xr, xr, dev_c),
-                send(fwd_label(k, 7), gr, gr, dev_c),
-            )
-        k = step - 1
-        if 0 <= k < experts:
-            at = rows(zs[k], core)
-            xx, gx = x.at[chip_x, at], g.at[chip_x, at]
-            xy, gy = x.at[chip_y, at], g.at[chip_y, at]
-            own[k][0].wait_recv()
-            dx = send(fwd_label(k, 8), xx, xx, dev_y)
-            own[k][1].wait_recv()
-            dg = send(fwd_label(k, 9), gy, gy, dev_x)
-            own[k][2].wait_recv()
-            own[k][3].wait_recv()
-            diag[k] = (dx, dg)
-            fromcore[1, k] = (
-                send(fwd_label(k, 10), xx, xx, dev_c),
-                send(fwd_label(k, 11), gx, gx, dev_c),
-            )
-            fromcore[2, k] = (
-                send(fwd_label(k, 12), xy, xy, dev_c),
-                send(fwd_label(k, 13), gy, gy, dev_c),
-            )
-        k = step - 2
-        if 0 <= k < experts:
-            at = rows(zs[k], core)
-            xd, gd = x.at[chip_d, at], g.at[chip_d, at]
-            diag[k][0].wait_recv()
-            diag[k][1].wait_recv()
-            fromcore[3, k] = (
-                send(fwd_label(k, 14), xd, xd, dev_c),
-                send(fwd_label(k, 15), gd, gd, dev_c),
-            )
-
-    for c in loads:
-        c.wait()
+
+    def spread(k):
+        if k > 0:
+            first[k][0].wait_recv()
+            first[k][1].wait_recv()
+            if k + 2 < experts:
+                exchange(k + 2)
+        at = rows(zs[k], core)
+        xr, gr = x.at[chip, at], g.at[chip, at]
+        own[k] = (
+            send(fwd_label(k, 2), xr, xr, dev_x),
+            send(fwd_label(k, 5), gr, gr, dev_y),
+            send(fwd_label(k, 3), gr, gr, dev_x),
+            send(fwd_label(k, 4), xr, xr, dev_y),
+        )
+        fromcore[0, k] = (
+            send(fwd_label(k, 6), xr, xr, dev_c),
+            send(fwd_label(k, 7), gr, gr, dev_c),
+        )
+
+    def relay(k):
+        at = rows(zs[k], core)
+        xx, gx = x.at[chip_x, at], g.at[chip_x, at]
+        xy, gy = x.at[chip_y, at], g.at[chip_y, at]
+        own[k][0].wait_recv()
+        dx = send(fwd_label(k, 8), xx, xx, dev_y)
+        own[k][1].wait_recv()
+        dg = send(fwd_label(k, 9), gy, gy, dev_x)
+        own[k][2].wait_recv()
+        own[k][3].wait_recv()
+        diag[k] = (dx, dg)
+        fromcore[1, k] = (
+            send(fwd_label(k, 10), xx, xx, dev_c),
+            send(fwd_label(k, 11), gx, gx, dev_c),
+        )
+        fromcore[2, k] = (
+            send(fwd_label(k, 12), xy, xy, dev_c),
+            send(fwd_label(k, 13), gy, gy, dev_c),
+        )
+
+    def relay_diag(k):
+        at = rows(zs[k], core)
+        xd, gd = x.at[chip_d, at], g.at[chip_d, at]
+        diag[k][0].wait_recv()
+        diag[k][1].wait_recv()
+        fromcore[3, k] = (
+            send(fwd_label(k, 14), xd, xd, dev_c),
+            send(fwd_label(k, 15), gd, gd, dev_c),
+        )
 
     tile = 512 if feats % 512 == 0 else LANES
     n_tiles = feats // tile
     chips = (chip, chip_x, chip_y, chip_d)
     back = experts * 16
     cores = {}
-    for q in (3, 1, 2, 0):
+
+    def compute(q):
         for k in range(experts):
             for c in fromcore[q, k]:
                 c.wait_recv()
@@ -257,22 +273,45 @@
 
     left = pl.ds(0, h1)
     right = pl.ds(h1, wide - h1)
-    back += 4
+    hops = back + 4
     hop1, hop2, home = {}, {}, {}
-    for q in (3, 1, 2):
+    mine_rows = pl.ds(pl.multiple_of(core * r, ROWS), r)
+
+    def add_core(q):
         cores[q].wait_recv()
+        t[chips[q], mine_rows, :] = (
+            t[chips[q], mine_rows, :].astype(F32) + rcore[q].astype(F32)
+        ).astype(BF16)
+
+    for step in range(experts):
+        spread(step)
+        if step >= 1:
+            relay(step - 1)
+        if step >= 2:
+            relay_diag(step - 2)
+    for c in loads:
+        c.wait()
+    compute(0)
+    relay(experts - 1)
+    relay_diag(experts - 2)
+    compute(1)
+    relay_diag(experts - 1)
+    compute(2)
+    add_core(1)
+    near_x = send(hops + 2, t.at[chip_x, mine_rows, left], rxa, dev_x)
+    add_core(2)
+    near_y = send(hops + 3, t.at[chip_y, mine_rows, right], rya, dev_y)
+    compute(3)
+    cores[3].wait_recv()
     for k in range(experts - 1, -1, -1):
         at, zk = rows(zs[k], core), slot(zs[k])
-        for q in (3, 1, 2):
-            t[chips[q], at, :] = (
-                t[chips[q], at, :].astype(F32) + rcore[q, zk, :].astype(F32)
-            ).astype(BF16)
-        b = back + 8 * k
+        t[chip_d, at, :] = (
+            t[chip_d, at, :].astype(F32) + rcore[3, zk, :].astype(F32)
+        ).astype(BF16)
+        b = hops + 8 * k
         hop1[k] = (
             send(b, t.at[chip_d, at, left], rxb.at[zk], dev_x),
             send(b + 1, t.at[chip_d, at, right], ryb.at[zk], dev_y),
-            send(b + 2, t.at[chip_x, at, left], rxa.at[zk], dev_x),
-            send(b + 3, t.at[chip_y, at, right], rya.at[zk], dev_y),
         )
 
     def wgrad(i, _):
@@ -285,7 +324,7 @@
     lax.fori_loop(0, n_tiles, wgrad, 0)
     for k in range(experts - 1, -1, -1):
         at, zk = rows(zs[k], core), slot(zs[k])
-        b = back + 8 * k
+        b = hops + 8 * k
         hop1[k][0].wait_recv()
         t[chip_y, at, left] = (t[chip_y, at, left].astype(F32) + rxb[zk, :].astype(F32)).astype(BF16)
         s1 = send(b + 4, t.at[chip_y, at, left], rf1.at[zk], dev_y)
@@ -301,9 +340,11 @@
 
     lax.fori_loop(0, n_tiles, dgrad, 0)
     cores[0].wait_recv()
+    near_x.wait_recv()
+    near_y.wait_recv()
     for k in range(experts - 1, -1, -1):
         at, zk = rows(zs[k], core), slot(zs[k])
-        for c in (hop1[k][2], hop1[k][3], hop2[k][0], hop2[k][1]):
+        for c in hop2[k]:
             c.wait_recv()
         mine = t[chip, at, :].astype(F32) + rcore[0, zk, :].astype(F32)
         lo = mine[:, :h1] + rxa[zk, :].astype(F32) + rf1[zk, :].astype(F32)
@@ -311,23 +352,45 @@
         if k > 0:
             t[chip, at, left] = lo.astype(BF16)
             t[chip, at, right] = hi.astype(BF16)
-            home[k] = send(back + 8 * k + 6, t.at[chip, at], o.at[slot(z)], dev_z[k])
+            home[k] = send(hops + 8 * k + 6, t.at[chip, at], o.at[slot(z)], dev_z[k])
         else:
             o[zk, left] = lo.astype(BF16)
             o[zk, right] = hi.astype(BF16)
     for k in range(1, experts):
         home[k].wait_recv()
-    out_tokens[...] = dot(place16, o[:, :feats], 1, 0).astype(BF16)
-    scores = o[:, feats:]
-    s0 = dot(jnp.where(on0, place, 0.0).astype(BF16), scores, 1, 0)
-    s1 = dot(jnp.where(on1, place, 0.0).astype(BF16), scores, 1, 0)
-    lane = lax.broadcasted_iota(jnp.int32, (toks, LANES), 1)
-    out_probs[...] = jnp.where(lane == 0, s0, s1)
+    out_tokens[...] = dot(place16, o[:, :feats], 0, 0).astype(BF16)
+    score = o[:, feats : feats + 1].astype(F32)
+    out_probs[0:1, :] = jnp.sum(jnp.where(on0, place, 0.0) * score, axis=0, keepdims=True)
+    out_probs[1:2, :] = jnp.sum(jnp.where(on1, place, 0.0) * score, axis=0, keepdims=True)
     for c in started:
         c.wait_send()
 
 
-def expert_call(experts, cap, tokens, grads, routes, probs, wg, wu, wd):
+def write_out(*refs):
+    count = len(refs) // 2
+    sems = refs[-1]
+    copies = [
+        pltpu.make_async_copy(refs[i], refs[count + i], sems.at[i]) for i in range(count)
+    ]
+    for c in copies:
+        c.start()
+    for c in copies:
+        c.wait()
+
+
+def finish(arrays):
+    arrays = [pltpu.with_memory_space_constraint(a, pltpu.VMEM) for a in arrays]
+    return pl.pallas_call(
+        write_out,
+        out_shape=[jax.ShapeDtypeStruct(a.shape, a.dtype) for a in arrays],
+        in_specs=[pl.BlockSpec(memory_space=pltpu.VMEM)] * len(arrays),
+        out_specs=[pl.BlockSpec(memory_space=pl.ANY)] * len(arrays),
+        scratch_shapes=[pltpu.SemaphoreType.DMA((len(arrays),))],
+        compiler_params=pltpu.CompilerParams(has_side_effects=True, vmem_limit_bytes=2**20),
+    )(*arrays)
+
+
+def expert_call(place, limit, experts, cap, tokens, grads, routes, probs, wg, wu, wd):
     toks, feats = tokens.shape
     hidden = wg.shape[1]
     r = experts * cap
@@ -335,19 +398,19 @@
     h1 = (wide // LANES + 1) // 2 * LANES
     h2 = wide - h1
     vmem = pl.BlockSpec(memory_space=pltpu.VMEM)
-    hbm = pl.BlockSpec(memory_space=pl.ANY)
+    hbm = pl.BlockSpec(memory_space=pltpu.HBM)
     n_sem = experts * 16 + 4 + 8 * experts
-    grad = jax.ShapeDtypeStruct((feats, hidden), BF16)
+    grad = place((feats, hidden), BF16)
     return pl.pallas_call(
         functools.partial(kernel, experts, cap),
         out_shape=(
-            jax.ShapeDtypeStruct((toks, feats), BF16),
-            jax.ShapeDtypeStruct((toks, LANES), F32),
+            place((toks, feats), BF16),
+            place((TOP, toks), F32),
             grad,
             grad,
             grad,
         ),
-        in_specs=[vmem] * 4 + [hbm] * 3,
+        in_specs=[hbm] * 7,
         out_specs=(vmem,) * 5,
         scratch_shapes=[
             pltpu.VMEM((r, wide), BF16),
@@ -368,12 +431,16 @@
             pltpu.VMEM((feats, hidden), BF16),
             pltpu.VMEM((2 * hidden, 8 * r), BF16),
             pltpu.VMEM((hidden, 8 * r), BF16),
-            pltpu.SemaphoreType.DMA((3,)),
+            pltpu.VMEM((toks, feats), BF16),
+            pltpu.VMEM((toks, feats), BF16),
+            pltpu.VMEM((TOP, toks), jnp.int32),
+            pltpu.VMEM((TOP, toks), F32),
+            pltpu.SemaphoreType.DMA((7,)),
             pltpu.SemaphoreType.DMA((n_sem,)),
             pltpu.SemaphoreType.DMA((n_sem,)),
         ],
         compiler_params=pltpu.CompilerParams(
-            collective_id=0, has_side_effects=True, vmem_limit_bytes=58 * 2**20
+            collective_id=0, has_side_effects=True, vmem_limit_bytes=limit
         ),
     )(tokens, grads, routes, probs, wg, wu, wd)
 
@@ -396,18 +463,21 @@
             term = lax.psum_scatter(term, "dp", scatter_dimension=0, tiled=True)
         return term.astype(BF16)[None]
 
-    grad_tokens, probs, gate, up, down = expert_call(
+    made = expert_call(
+        jax.ShapeDtypeStruct if split else pltpu.VMEM,
+        58 * 2**20 if split else 64100000,
         experts,
         cap,
         tokens,
         grad_out,
-        routes,
-        route_probs,
+        routes.T,
+        route_probs.T,
         whole(gate_weight),
         whole(up_weight),
         whole(down_weight),
     )
-    return (grad_tokens, probs[:, :TOP], shared(gate), shared(up), shared(down))
+    grad_tokens, probs, gate, up, down = made if split else finish(made)
+    return (grad_tokens, probs.T, shared(gate), shared(up), shared(down))
 
 
 def solution(mesh):

time: 91.6 us -> 74 us (0.81)
  local copies, waits for them, and re-layouts: 9.65 us -> 0 us
  Pallas kernels: 80.9 us -> 73.2 us
    unnamed x17 -> x0, local copies, waits for them, and re-layouts: 9.65 us -> none
    pallas_call x1 -> x2, Pallas kernels: 80.9 us -> 73.2 us  [the longest x1 71.5 us: expert_call(): pl.pallas_call(functools.partial(kernel, experts, cap), out_shape=(place(...]
where the time goes in v2:
time: 74 us; the launch traced here: 73.8 us
  Pallas kernels  73.2 us (99%)
    pallas_call x1, Pallas kernels, expert_call(): pl.pallas_call(functools.partial(kernel, experts, cap), out_shape=(place(...  71.5 us
    pallas_call x1, Pallas kernels, finish(): pl.pallas_call(write_out, out_shape=[jax.ShapeDtypeStruct(a.shape, a.dtyp...  1.63 us

profile of v2, /device:TPU:0, one launch (start us, length us, event | category | flops | bytes accessed | tf_op | source)
XLA Modules:
  0.0 73.8 jit_solution(475370470993948266)
XLA Ops:
  0.6 71.5 %shard_map.110 = (bf16[24,3584]{1,0:T(8,128)(2,1)S(1)}, f32[2,24]{1,0:T(2,128)S(1)}, bf16[3584,128]{1,0:T(8,128)(2,1)S(1)}, bf16[3584,128]{1,0:T(8,128)(2,1)S(1)}, bf16[3584,128]{1,0:T(8,128)(2,1)S(1)}) custom-call(bf16[24,3584]{1,0:T(8,128)(2,1)} %tokens_hbm.1, bf16[24,3584]{1,0:T(8,128)(2,1)} %grads_hbm.1, s32[2,24]{1,0:T(2,128)} %bitcast.12, ...), custom_call_target="tpu_custom_call" | custom-call | tf_op jit(solution)/shard_map/pallas_call | solution.py:404
  72.2 1.6 %shard_map.111 = (bf16[24,3584]{1,0:T(8,128)(2,1)}, f32[2,24]{1,0:T(2,128)}, bf16[3584,128]{1,0:T(8,128)(2,1)}, bf16[3584,128]{1,0:T(8,128)(2,1)}, bf16[3584,128]{1,0:T(8,128)(2,1)}) custom-call(bf16[24,3584]{1,0:T(8,128)(2,1)S(1)} %get-tuple-element.15.refs_0_, f32[2,24]{1,0:T(2,128)S(1)} %get-tuple-element.16.refs_1_, ...), custom_call_target="tpu_custom_call" | custom-call | tf_op jit(solution)/shard_map/pallas_call | solution.py:383

commit v3 on v2

--- a/solution.py
+++ b/solution.py
@@ -43,7 +43,6 @@
     gs,
     x,
     g,
-    sc,
     t,
     rcore,
     rxa,
@@ -264,7 +263,6 @@
         def part(i, _):
             at = pl.ds(pl.multiple_of(i * tile, tile), tile)
             t[cq, :, at] = dot(both, wgu[at, :], 1, 1).astype(BF16)
-            sc[cq, :, at] = (prob * g[cq, :, at].astype(F32)).astype(BF16)
             return 0
 
         lax.fori_loop(0, n_tiles, part, 0)
@@ -333,9 +331,13 @@
         s2 = send(b + 5, t.at[chip_x, at, right], rf2.at[zk], dev_x)
         hop2[k] = (s1, s2)
 
+    tails = x[:, :, feats:].reshape(8 * r, LANES).astype(F32)
+    row_prob = tails[:, 0:1] + tails[:, LANES // 2 : LANES // 2 + 1]
+
     def dgrad(i, _):
         at = pl.ds(pl.multiple_of(i * tile, tile), tile)
-        out_down[at, :] = dot(hid[...], sc[:, :, at].reshape(8 * r, tile), 1, 0).astype(BF16).T
+        scaled = (row_prob * g[:, :, at].reshape(8 * r, tile).astype(F32)).astype(BF16)
+        out_down[at, :] = dot(hid[...], scaled, 1, 0).astype(BF16).T
         return 0
 
     lax.fori_loop(0, n_tiles, dgrad, 0)
@@ -417,7 +419,6 @@
             pltpu.VMEM((r, feats), BF16),
             pltpu.VMEM((4, 2 * r, wide), BF16),
             pltpu.VMEM((4, 2 * r, feats), BF16),
-            pltpu.VMEM((4, 2 * r, feats), BF16),
             pltpu.VMEM((4, 2 * r, wide), BF16),
             pltpu.VMEM((4, r, wide), BF16),
             pltpu.VMEM((r, h1), BF16),

time: 74 us -> 74.7 us (level)
  no operation moved by 1% of the time
where the time goes in v3:
time: 74.7 us; the launch traced here: 74.5 us
  Pallas kernels  73.9 us (99%)
    pallas_call x1, Pallas kernels, expert_call(): pl.pallas_call(functools.partial(kernel, experts, cap), out_shape=(place(...  72.2 us
    pallas_call x1, Pallas kernels, finish(): pl.pallas_call(write_out, out_shape=[jax.ShapeDtypeStruct(a.shape, a.dtyp...  1.63 us

profile of v3, /device:TPU:0, one launch (start us, length us, event | category | flops | bytes accessed | tf_op | source)
XLA Modules:
  0.0 74.5 jit_solution(5289376176673347410)
XLA Ops:
  0.6 72.2 %shard_map.110 = (bf16[24,3584]{1,0:T(8,128)(2,1)S(1)}, f32[2,24]{1,0:T(2,128)S(1)}, bf16[3584,128]{1,0:T(8,128)(2,1)S(1)}, bf16[3584,128]{1,0:T(8,128)(2,1)S(1)}, bf16[3584,128]{1,0:T(8,128)(2,1)S(1)}) custom-call(bf16[24,3584]{1,0:T(8,128)(2,1)} %tokens_hbm.1, bf16[24,3584]{1,0:T(8,128)(2,1)} %grads_hbm.1, s32[2,24]{1,0:T(2,128)} %bitcast.12, ...), custom_call_target="tpu_custom_call" | custom-call | tf_op jit(solution)/shard_map/pallas_call | solution.py:406
  72.9 1.6 %shard_map.111 = (bf16[24,3584]{1,0:T(8,128)(2,1)}, f32[2,24]{1,0:T(2,128)}, bf16[3584,128]{1,0:T(8,128)(2,1)}, bf16[3584,128]{1,0:T(8,128)(2,1)}, bf16[3584,128]{1,0:T(8,128)(2,1)}) custom-call(bf16[24,3584]{1,0:T(8,128)(2,1)S(1)} %get-tuple-element.15.refs_0_, f32[2,24]{1,0:T(2,128)S(1)} %get-tuple-element.16.refs_1_, ...), custom_call_target="tpu_custom_call" | custom-call | tf_op jit(solution)/shard_map/pallas_call | solution.py:385
